TPU v7x, 512 devices: a whole 4x4x16 slice. The times are simulated.
512 devices in a mesh: gx: 4 (over y), gy: 4 (over z_hi, core), gz: 32 (over z_lo, x).
Axes of the slice: x: 4, y: 4, z: 16 (z_hi: 2, z_lo: 8; z = z_hi * 8 + z_lo), core: 2. Of those that a mesh axis runs over, the one named last changes fastest.
Arguments:
- density: float32 [256, 256, 256], P(('gx', 'gz'), 'gy'), may hold values from 0.5 to 2
- pheromone: float32 [256, 256, 256], P(('gx', 'gz'), 'gy'), may hold values from -6 to 6
Outputs:
- new_density: float32 [256, 256, 256], P(('gx', 'gz'), 'gy')
- new_pheromone: float32 [256, 256, 256], P(('gx', 'gz'), 'gy')
All inputs are finite; a program needn't handle non-finite values.
Results may differ from a plain program's by a relative error of at most 0.0003.
Values sent between devices are 32-bit elements; how exact they have to be, the bound alone decides.
A program may use at most 64 MiB of HBM per device.

v0:
```python
import math

import jax
import jax.numpy as jnp
from jax import lax
from jax.sharding import PartitionSpec as P

NX = 256
NY = 256
NZ = 256


step_chemo = 0.0001
step_motile = 0.0002
step_diffuse = 0.0002
step_secrete = 0.5
step_decay = 0.1


def angle_table(length, sign):
    places = jnp.arange(length, dtype=jnp.int32)
    angle = (places[:, None] * places[None, :] % length).astype(jnp.float32) * (
        2.0 * math.pi / length
    )
    return (jnp.cos(angle), sign * jnp.sin(angle))


def times_right(field, table):
    return jnp.matmul(field, table, precision=lax.Precision.HIGHEST)


def times_left(table, field):
    return jnp.matmul(table, field, precision=lax.Precision.HIGHEST)


def last_dft(real_part, imag_part, sign):
    cosine, sine = angle_table(real_part.shape[-1], sign)
    if imag_part is None:
        return (times_right(real_part, cosine), times_right(real_part, sine))
    out_real = times_right(real_part, cosine) - times_right(imag_part, sine)
    return (out_real, None)


def middle_dft(real_part, imag_part, sign):
    cosine, sine = angle_table(real_part.shape[1], sign)
    out_real = times_left(cosine, real_part) - times_left(sine, imag_part)
    out_imag = times_left(cosine, imag_part) + times_left(sine, real_part)
    return (out_real, out_imag)


def deriv_numbers(places, length):
    signed = jnp.where(places < length // 2, places, places - length)
    deriv = jnp.where(places == length // 2, 0, signed)
    return (signed.astype(jnp.float32), deriv.astype(jnp.float32))


def brick_to_lines(field, groups):
    count, x_local, y_local, z_full = field.shape
    z_local = z_full // groups
    moved = field.reshape(count, x_local, y_local, groups, z_local).transpose(0, 3, 2, 1, 4)
    return moved.reshape(count, groups, 1, y_local * x_local * z_local)


def after_lines(field, y_local):
    count, unused, groups, width = field.shape
    return field.reshape(count, groups * y_local, width // y_local)


def lines_to_brick(field, groups):
    count, y_full, width = field.shape
    return field.reshape(count, groups, 1, y_full // groups * width)


def after_brick(field, y_local, x_local):
    count, unused, groups, width = field.shape
    z_local = width // (y_local * x_local)
    moved = field.reshape(count, groups, y_local, x_local, z_local).transpose(0, 3, 2, 1, 4)
    return moved.reshape(count, x_local, y_local, groups * z_local)


def lines_to_pencil(field, peers, x_local):
    count, y_full, width = field.shape
    y_inner = y_full // peers
    z_local = width // x_local
    moved = field.reshape(count, peers, y_inner, x_local, z_local).transpose(0, 1, 3, 2, 4)
    return moved.reshape(count, peers, 1, x_local * y_inner * z_local)


def after_pencil(field, x_local):
    count, unused, peers, width = field.shape
    return field.reshape(count, peers * x_local, width // x_local)


def pencil_to_lines(field, peers):
    count, x_full, width = field.shape
    return field.reshape(count, peers, 1, x_full // peers * width)


def after_back(field, x_local, z_local):
    count, unused, peers, width = field.shape
    y_inner = width // (x_local * z_local)
    moved = field.reshape(count, peers, x_local, y_inner, z_local).transpose(0, 1, 3, 2, 4)
    return moved.reshape(count, peers * y_inner, x_local * z_local)


def forward(fields):
    count, x_local, y_local, z_full = fields.shape
    groups = lax.axis_size("gy")
    peers = lax.axis_size("gx") * lax.axis_size("gz")
    real_part, imag_part = last_dft(fields.reshape(count, x_local * y_local, z_full), None, -1.0)
    real_part = brick_to_lines(real_part.reshape(fields.shape), groups)
    imag_part = brick_to_lines(imag_part.reshape(fields.shape), groups)
    real_part, imag_part = (
        lax.all_to_all(real_part, "gy", split_axis=1, concat_axis=2, tiled=True),
        lax.all_to_all(imag_part, "gy", split_axis=1, concat_axis=2, tiled=True),
    )
    real_part, imag_part = middle_dft(
        after_lines(real_part, y_local), after_lines(imag_part, y_local), -1.0
    )
    real_part = lines_to_pencil(real_part, peers, x_local)
    imag_part = lines_to_pencil(imag_part, peers, x_local)
    real_part, imag_part = (
        lax.all_to_all(real_part, ("gx", "gz"), split_axis=1, concat_axis=2, tiled=True),
        lax.all_to_all(imag_part, ("gx", "gz"), split_axis=1, concat_axis=2, tiled=True),
    )
    return middle_dft(after_pencil(real_part, x_local), after_pencil(imag_part, x_local), -1.0)


def inverse(real_part, imag_part, x_local, y_local):
    groups = lax.axis_size("gy")
    peers = lax.axis_size("gx") * lax.axis_size("gz")
    z_local = NZ // groups
    real_part, imag_part = middle_dft(real_part, imag_part, 1.0)
    real_part = pencil_to_lines(real_part, peers)
    imag_part = pencil_to_lines(imag_part, peers)
    real_part, imag_part = (
        lax.all_to_all(real_part, ("gx", "gz"), split_axis=1, concat_axis=2, tiled=True),
        lax.all_to_all(imag_part, ("gx", "gz"), split_axis=1, concat_axis=2, tiled=True),
    )
    real_part = after_back(real_part, x_local, z_local)
    imag_part = after_back(imag_part, x_local, z_local)
    real_part, imag_part = middle_dft(real_part, imag_part, 1.0)
    real_part = lines_to_brick(real_part, groups)
    imag_part = lines_to_brick(imag_part, groups)
    real_part, imag_part = (
        lax.all_to_all(real_part, "gy", split_axis=1, concat_axis=2, tiled=True),
        lax.all_to_all(imag_part, "gy", split_axis=1, concat_axis=2, tiled=True),
    )
    real_part = after_brick(real_part, y_local, x_local)
    imag_part = after_brick(imag_part, y_local, x_local)
    count = real_part.shape[0]
    flat_real = real_part.reshape(count, x_local * y_local, NZ)
    flat_imag = imag_part.reshape(count, x_local * y_local, NZ)
    result, unused = last_dft(flat_real, flat_imag, 1.0)
    return result.reshape(count, x_local, y_local, NZ) * (1.0 / (NX * NY * NZ))


def per_device(density, pheromone):
    x_local, y_local, z_full = density.shape
    groups = lax.axis_size("gy")
    z_local = z_full // groups
    real_part, imag_part = forward(jnp.stack([density, pheromone]))
    yz_width = real_part.shape[2]
    y_inner = yz_width // z_local
    block = lax.axis_index("gx") * lax.axis_size("gz") + lax.axis_index("gz")
    columns = jnp.arange(yz_width, dtype=jnp.int32)
    places_x = jnp.arange(NX, dtype=jnp.int32)
    places_y = block * y_inner + columns // z_local
    places_z = lax.axis_index("gy") * z_local + columns % z_local
    signed_x, deriv_x = deriv_numbers(places_x, NX)
    signed_y, deriv_y = deriv_numbers(places_y, NY)
    signed_z, deriv_z = deriv_numbers(places_z, NZ)
    signed_x, deriv_x = (signed_x[:, None], deriv_x[:, None])
    signed_y, deriv_y = (signed_y[None, :], deriv_y[None, :])
    signed_z, deriv_z = (signed_z[None, :], deriv_z[None, :])
    ksquare = signed_x * signed_x + signed_y * signed_y + signed_z * signed_z
    motile = 1.0 / (1.0 + step_motile * ksquare)
    diffuse = 1.0 / (1.0 + step_diffuse * ksquare + step_decay)
    dens_real, phero_real = (real_part[0], real_part[1])
    dens_imag, phero_imag = (imag_part[0], imag_part[1])
    grad_real = jnp.stack([-deriv_x * phero_imag, -deriv_y * phero_imag, -deriv_z * phero_imag])
    grad_imag = jnp.stack([deriv_x * phero_real, deriv_y * phero_real, deriv_z * phero_real])
    gradient = inverse(grad_real, grad_imag, x_local, y_local)
    flux_real, flux_imag = forward(density[None] * gradient)
    div_real = -(deriv_x * flux_imag[0] + deriv_y * flux_imag[1] + deriv_z * flux_imag[2])
    div_imag = deriv_x * flux_real[0] + deriv_y * flux_real[1] + deriv_z * flux_real[2]
    new_dens_real = (dens_real - step_chemo * div_real) * motile
    new_dens_imag = (dens_imag - step_chemo * div_imag) * motile
    new_phero_real = (phero_real + step_secrete * dens_real) * diffuse
    new_phero_imag = (phero_imag + step_secrete * dens_imag) * diffuse
    fields = inverse(
        jnp.stack([new_dens_real, new_phero_real]),
        jnp.stack([new_dens_imag, new_phero_imag]),
        x_local,
        y_local,
    )
    return (fields[0], fields[1])


def solution(mesh):
    placed = (P(("gx", "gz"), "gy", None), P(("gx", "gz"), "gy", None))
    return jax.shard_map(
        per_device,
        mesh=mesh,
        in_specs=placed,
        out_specs=(P(("gx", "gz"), "gy", None), P(("gx", "gz"), "gy", None)),
        check_vma=False,
    )
```

profile of v0, /device:TPU:33, one launch (start us, length us, event | category | flops | bytes accessed | tf_op | source)
XLA Modules:
  0.0 522.6 jit_solution(15989248999031217807)
XLA Ops:
  0.6 2.6 convolution_bitcast_fusion.3
  4.8 15.0 %all-to-all-start = ((f32[2,4,1,8192]{3,0,2,1:T(2,128)}), f32[2,4,1,8192]{3,0,2,1:T(2,128)S(1)}, u32[]{:S(2)}, u32[]{:S(2)}) async-start(f32[2,4,1,8192]{3,0,2,1:T(2,128)} %reshape.658), calls=%async_computation | async-start | bytes 524288 | tf_op jit(solution)/shard_map/all_to_all | solution.py:114
  19.8 1.6 convolution_bitcast_fusion.2
  23.0 19.1 %all-to-all-done = f32[2,4,1,8192]{3,0,2,1:T(2,128)S(1)} async-done(((f32[2,4,1,8192]{3,0,2,1:T(2,128)}), f32[2,4,1,8192]{3,0,2,1:T(2,128)S(1)}, u32[]{:S(2)}, u32[]{:S(2)}) %all-to-all-start) | async-done | bytes 262176 | tf_op jit(solution)/shard_map/all_to_all | solution.py:114
  42.1 4.2 all-to-all-start.1
  46.7 1.6 fusion.81
  48.3 15.3 %all-to-all-done.1 = f32[2,4,1,8192]{3,0,2,1:T(2,128)S(1)} async-done(((f32[2,4,1,8192]{3,0,2,1:T(2,128)}), f32[2,4,1,8192]{3,0,2,1:T(2,128)S(1)}, u32[]{:S(2)}, u32[]{:S(2)}) %all-to-all-start.1) | async-done | bytes 262176 | tf_op jit(solution)/shard_map/all_to_all | solution.py:115
  64.0 1.6 fusion.17
  67.0 12.8 %all-to-all-start.2 = ((f32[2,128,1,256]{3,0,2,1:T(2,128)}), f32[2,128,1,256]{3,0,2,1:T(2,128)S(1)}, u32[]{:S(2)}, u32[]{:S(2)}) async-start(f32[2,128,1,256]{3,0,2,1:T(2,128)} %copy.133), calls=%async_computation.2 | async-start | bytes 524288 | tf_op jit(solution)/shard_map/all_to_all | solution.py:123
  79.8 1.6 fusion.77
  81.4 1.6 fusion.16
  84.4 14.2 %all-to-all-done.2 = f32[2,128,1,256]{3,0,2,1:T(2,128)S(1)} async-done(((f32[2,128,1,256]{3,0,2,1:T(2,128)}), f32[2,128,1,256]{3,0,2,1:T(2,128)S(1)}, u32[]{:S(2)}, u32[]{:S(2)}) %all-to-all-start.2) | async-done | bytes 262176 | tf_op jit(solution)/shard_map/all_to_all | solution.py:123
  98.6 9.2 %all-to-all-start.3 = ((f32[2,128,1,256]{3,0,2,1:T(2,128)}), f32[2,128,1,256]{3,0,2,1:T(2,128)S(1)}, u32[]{:S(2)}, u32[]{:S(2)}) async-start(f32[2,128,1,256]{3,0,2,1:T(2,128)} %copy.136), calls=%async_computation.3 | async-start | bytes 524288 | tf_op jit(solution)/shard_map/all_to_all | solution.py:124
  108.4 1.6 fusion.79
  110.0 16.6 %all-to-all-done.3 = f32[2,128,1,256]{3,0,2,1:T(2,128)S(1)} async-done(((f32[2,128,1,256]{3,0,2,1:T(2,128)}), f32[2,128,1,256]{3,0,2,1:T(2,128)S(1)}, u32[]{:S(2)}, u32[]{:S(2)}) %all-to-all-start.3) | async-done | bytes 262176 | tf_op jit(solution)/shard_map/all_to_all | solution.py:124
  126.7 1.6 fusion.75
  128.3 1.6 fusion.15
  129.9 1.6 fusion.14
  131.7 1.6 fusion.18
  133.4 1.6 fusion.6
  136.3 9.1 %all-to-all-start.5 = ((f32[3,128,1,256]{3,2,0,1:T(1,128)}), f32[3,128,1,256]{3,2,0,1:T(1,128)S(1)}, u32[]{:S(2)}, u32[]{:S(2)}) async-start(f32[3,128,1,256]{3,2,0,1:T(1,128)} %copy.141), calls=%async_computation.5 | async-start | bytes 786432 | tf_op jit(solution)/shard_map/all_to_all | solution.py:138
  145.4 1.6 fusion.19
  147.0 1.6 fusion.7
  149.9 20.0 %all-to-all-done.5 = f32[3,128,1,256]{3,2,0,1:T(1,128)S(1)} async-done(((f32[3,128,1,256]{3,2,0,1:T(1,128)}), f32[3,128,1,256]{3,2,0,1:T(1,128)S(1)}, u32[]{:S(2)}, u32[]{:S(2)}) %all-to-all-start.5) | async-done | bytes 393248 | tf_op jit(solution)/shard_map/all_to_all | solution.py:138
  169.8 9.1 %all-to-all-start.4 = ((f32[3,128,1,256]{3,2,0,1:T(1,128)}), f32[3,128,1,256]{3,2,0,1:T(1,128)S(1)}, u32[]{:S(2)}, u32[]{:S(2)}) async-start(f32[3,128,1,256]{3,2,0,1:T(1,128)} %copy.138), calls=%async_computation.4 | async-start | bytes 786432 | tf_op jit(solution)/shard_map/all_to_all | solution.py:137
  180.6 1.6 fusion.67
  182.2 21.0 %all-to-all-done.4 = f32[3,128,1,256]{3,2,0,1:T(1,128)S(1)} async-done(((f32[3,128,1,256]{3,2,0,1:T(1,128)}), f32[3,128,1,256]{3,2,0,1:T(1,128)S(1)}, u32[]{:S(2)}, u32[]{:S(2)}) %all-to-all-start.4) | async-done | bytes 393248 | tf_op jit(solution)/shard_map/all_to_all | solution.py:137
  204.8 1.6 fusion.4
  207.7 5.6 %all-to-all-start.7 = ((f32[3,4,1,8192]{3,2,0,1:T(1,128)}), f32[3,4,1,8192]{3,2,0,1:T(1,128)S(1)}, u32[]{:S(2)}, u32[]{:S(2)}) async-start(f32[3,4,1,8192]{3,2,0,1:T(1,128)} %copy.147), calls=%async_computation.7 | async-start | bytes 786432 | tf_op jit(solution)/shard_map/all_to_all | solution.py:147
  213.4 1.6 fusion.72
  215.0 1.6 fusion.5
  217.9 23.4 %all-to-all-done.7 = f32[3,4,1,8192]{3,2,0,1:T(1,128)S(1)} async-done(((f32[3,4,1,8192]{3,2,0,1:T(1,128)}), f32[3,4,1,8192]{3,2,0,1:T(1,128)S(1)}, u32[]{:S(2)}, u32[]{:S(2)}) %all-to-all-start.7) | async-done | bytes 393248 | tf_op jit(solution)/shard_map/all_to_all | solution.py:147
  241.3 4.7 all-to-all-start.6
  249.1 15.6 %all-to-all-done.6 = f32[3,4,1,8192]{3,2,0,1:T(1,128)S(1)} async-done(((f32[3,4,1,8192]{3,2,0,1:T(1,128)}), f32[3,4,1,8192]{3,2,0,1:T(1,128)S(1)}, u32[]{:S(2)}, u32[]{:S(2)}) %all-to-all-start.6) | async-done | bytes 393248 | tf_op jit(solution)/shard_map/all_to_all | solution.py:146
  270.9 1.6 reshape.660
  272.5 6.2 %all-to-all-start.8 = ((f32[3,4,1,8192]{3,2,0,1:T(1,128)}), f32[3,4,1,8192]{3,2,0,1:T(1,128)S(1)}, u32[]{:S(2)}, u32[]{:S(2)}) async-start(f32[3,4,1,8192]{3,2,0,1:T(1,128)} %reshape.660), calls=%async_computation.8 | async-start | bytes 786432 | tf_op jit(solution)/shard_map/all_to_all | solution.py:115
  280.2 1.6 reshape.661
  281.7 12.7 %all-to-all-done.8 = f32[3,4,1,8192]{3,2,0,1:T(1,128)S(1)} async-done(((f32[3,4,1,8192]{3,2,0,1:T(1,128)}), f32[3,4,1,8192]{3,2,0,1:T(1,128)S(1)}, u32[]{:S(2)}, u32[]{:S(2)}) %all-to-all-start.8) | async-done | bytes 393248 | tf_op jit(solution)/shard_map/all_to_all | solution.py:115
  294.4 4.2 all-to-all-start.9
  299.1 1.6 fusion.65
  300.7 15.1 %all-to-all-done.9 = f32[3,4,1,8192]{3,2,0,1:T(1,128)S(1)} async-done(((f32[3,4,1,8192]{3,2,0,1:T(1,128)}), f32[3,4,1,8192]{3,2,0,1:T(1,128)S(1)}, u32[]{:S(2)}, u32[]{:S(2)}) %all-to-all-start.9) | async-done | bytes 393248 | tf_op jit(solution)/shard_map/all_to_all | solution.py:114
  316.4 1.6 fusion.3
  320.2 20.6 %all-to-all-start.10 = ((f32[3,128,1,256]{3,2,0,1:T(1,128)}), f32[3,128,1,256]{3,2,0,1:T(1,128)S(1)}, u32[]{:S(2)}, u32[]{:S(2)}) async-start(f32[3,128,1,256]{3,2,0,1:T(1,128)} %copy.157), calls=%async_computation.10 | async-start | bytes 786432 | tf_op jit(solution)/shard_map/all_to_all | solution.py:124
  340.8 1.6 fusion.61
  342.4 1.6 fusion.2
  346.1 19.2 %all-to-all-done.10 = f32[3,128,1,256]{3,2,0,1:T(1,128)S(1)} async-done(((f32[3,128,1,256]{3,2,0,1:T(1,128)}), f32[3,128,1,256]{3,2,0,1:T(1,128)S(1)}, u32[]{:S(2)}, u32[]{:S(2)}) %all-to-all-start.10) | async-done | bytes 393248 | tf_op jit(solution)/shard_map/all_to_all | solution.py:124
  365.3 9.3 %all-to-all-start.11 = ((f32[3,128,1,256]{3,2,0,1:T(1,128)}), f32[3,128,1,256]{3,2,0,1:T(1,128)S(1)}, u32[]{:S(2)}, u32[]{:S(2)}) async-start(f32[3,128,1,256]{3,2,0,1:T(1,128)} %copy.160), calls=%async_computation.11 | async-start | bytes 786432 | tf_op jit(solution)/shard_map/all_to_all | solution.py:123
  374.7 1.6 fusion.63
  376.3 22.7 %all-to-all-done.11 = f32[3,128,1,256]{3,2,0,1:T(1,128)S(1)} async-done(((f32[3,128,1,256]{3,2,0,1:T(1,128)}), f32[3,128,1,256]{3,2,0,1:T(1,128)S(1)}, u32[]{:S(2)}, u32[]{:S(2)}) %all-to-all-start.11) | async-done | bytes 393248 | tf_op jit(solution)/shard_map/all_to_all | solution.py:123
  399.0 1.6 fusion.57
  400.6 1.6 fusion.1
  402.2 1.6 fusion
  408.4 9.2 %all-to-all-start.13 = ((f32[2,128,1,256]{3,0,2,1:T(2,128)}), f32[2,128,1,256]{3,0,2,1:T(2,128)S(1)}, u32[]{:S(2)}, u32[]{:S(2)}) async-start(f32[2,128,1,256]{3,0,2,1:T(2,128)} %copy.165), calls=%async_computation.13 | async-start | bytes 524288 | tf_op jit(solution)/shard_map/all_to_all | solution.py:138
  421.3 15.0 %all-to-all-done.13 = f32[2,128,1,256]{3,0,2,1:T(2,128)S(1)} async-done(((f32[2,128,1,256]{3,0,2,1:T(2,128)}), f32[2,128,1,256]{3,0,2,1:T(2,128)S(1)}, u32[]{:S(2)}, u32[]{:S(2)}) %all-to-all-start.13) | async-done | bytes 262176 | tf_op jit(solution)/shard_map/all_to_all | solution.py:138
  436.3 9.1 %all-to-all-start.12 = ((f32[2,128,1,256]{3,0,2,1:T(2,128)}), f32[2,128,1,256]{3,0,2,1:T(2,128)S(1)}, u32[]{:S(2)}, u32[]{:S(2)}) async-start(f32[2,128,1,256]{3,0,2,1:T(2,128)} %copy.162), calls=%async_computation.12 | async-start | bytes 524288 | tf_op jit(solution)/shard_map/all_to_all | solution.py:137
  446.2 1.6 fusion.49
  447.8 16.5 %all-to-all-done.12 = f32[2,128,1,256]{3,0,2,1:T(2,128)S(1)} async-done(((f32[2,128,1,256]{3,0,2,1:T(2,128)}), f32[2,128,1,256]{3,0,2,1:T(2,128)S(1)}, u32[]{:S(2)}, u32[]{:S(2)}) %all-to-all-start.12) | async-done | bytes 262176 | tf_op jit(solution)/shard_map/all_to_all | solution.py:137
  465.1 1.6 fusion.10
  467.7 5.9 %all-to-all-start.15 = ((f32[2,4,1,8192]{3,0,2,1:T(2,128)}), f32[2,4,1,8192]{3,0,2,1:T(2,128)S(1)}, u32[]{:S(2)}, u32[]{:S(2)}) async-start(f32[2,4,1,8192]{3,0,2,1:T(2,128)} %copy.170), calls=%async_computation.15 | async-start | bytes 524288 | tf_op jit(solution)/shard_map/all_to_all | solution.py:147
  473.7 1.6 fusion.55
  475.3 1.6 fusion.11
  477.9 18.2 %all-to-all-done.15 = f32[2,4,1,8192]{3,0,2,1:T(2,128)S(1)} async-done(((f32[2,4,1,8192]{3,0,2,1:T(2,128)}), f32[2,4,1,8192]{3,0,2,1:T(2,128)S(1)}, u32[]{:S(2)}, u32[]{:S(2)}) %all-to-all-start.15) | async-done | bytes 262176 | tf_op jit(solution)/shard_map/all_to_all | solution.py:147
  496.1 4.4 all-to-all-start.14
  501.7 15.9 %all-to-all-done.14 = f32[2,4,1,8192]{3,0,2,1:T(2,128)S(1)} async-done(((f32[2,4,1,8192]{3,0,2,1:T(2,128)}), f32[2,4,1,8192]{3,0,2,1:T(2,128)S(1)}, u32[]{:S(2)}, u32[]{:S(2)}) %all-to-all-start.14) | async-done | bytes 262176 | tf_op jit(solution)/shard_map/all_to_all | solution.py:146
  (106 shorter events, 49.2 us)
Async XLA Ops:
  4.8 15.0 %copy-start = (f32[2,64,256]{2,1,0:T(8,128)S(1)}, f32[2,64,256]{2,1,0:T(8,128)}, u32[]{:S(2)}) copy-start(f32[2,64,256]{2,1,0:T(8,128)} %param.2) | copy-start | bytes 393220
  4.8 15.0 %copy-start.2 = (f32[2,64,256]{2,1,0:T(8,128)S(1)}, f32[2,64,256]{2,1,0:T(8,128)}, u32[]{:S(2)}) copy-start(f32[2,64,256]{2,1,0:T(8,128)} %param.3) | copy-start | bytes 393220
  4.8 37.3 %all-to-all-start = ((f32[2,4,1,8192]{3,0,2,1:T(2,128)}), f32[2,4,1,8192]{3,0,2,1:T(2,128)S(1)}, u32[]{:S(2)}, u32[]{:S(2)}) async-start(f32[2,4,1,8192]{3,0,2,1:T(2,128)} %reshape.658), calls=%async_computation | async-start | bytes 524288 | tf_op jit(solution)/shard_map/all_to_all | solution.py:114
  42.1 21.5 %all-to-all-start.1 = ((f32[2,4,1,8192]{3,0,2,1:T(2,128)}), f32[2,4,1,8192]{3,0,2,1:T(2,128)S(1)}, u32[]{:S(2)}, u32[]{:S(2)}) async-start(f32[2,4,1,8192]{3,0,2,1:T(2,128)} %reshape.659), calls=%async_computation.1 | async-start | bytes 524288 | tf_op jit(solution)/shard_map/all_to_all | solution.py:115
  67.0 31.6 %all-to-all-start.2 = ((f32[2,128,1,256]{3,0,2,1:T(2,128)}), f32[2,128,1,256]{3,0,2,1:T(2,128)S(1)}, u32[]{:S(2)}, u32[]{:S(2)}) async-start(f32[2,128,1,256]{3,0,2,1:T(2,128)} %copy.133), calls=%async_computation.2 | async-start | bytes 524288 | tf_op jit(solution)/shard_map/all_to_all | solution.py:123
  98.6 28.1 %all-to-all-start.3 = ((f32[2,128,1,256]{3,0,2,1:T(2,128)}), f32[2,128,1,256]{3,0,2,1:T(2,128)S(1)}, u32[]{:S(2)}, u32[]{:S(2)}) async-start(f32[2,128,1,256]{3,0,2,1:T(2,128)} %copy.136), calls=%async_computation.3 | async-start | bytes 524288 | tf_op jit(solution)/shard_map/all_to_all | solution.py:124
  136.3 33.6 %all-to-all-start.5 = ((f32[3,128,1,256]{3,2,0,1:T(1,128)}), f32[3,128,1,256]{3,2,0,1:T(1,128)S(1)}, u32[]{:S(2)}, u32[]{:S(2)}) async-start(f32[3,128,1,256]{3,2,0,1:T(1,128)} %copy.141), calls=%async_computation.5 | async-start | bytes 786432 | tf_op jit(solution)/shard_map/all_to_all | solution.py:138
  169.8 33.3 %all-to-all-start.4 = ((f32[3,128,1,256]{3,2,0,1:T(1,128)}), f32[3,128,1,256]{3,2,0,1:T(1,128)S(1)}, u32[]{:S(2)}, u32[]{:S(2)}) async-start(f32[3,128,1,256]{3,2,0,1:T(1,128)} %copy.138), calls=%async_computation.4 | async-start | bytes 786432 | tf_op jit(solution)/shard_map/all_to_all | solution.py:137
  207.7 33.6 %all-to-all-start.7 = ((f32[3,4,1,8192]{3,2,0,1:T(1,128)}), f32[3,4,1,8192]{3,2,0,1:T(1,128)S(1)}, u32[]{:S(2)}, u32[]{:S(2)}) async-start(f32[3,4,1,8192]{3,2,0,1:T(1,128)} %copy.147), calls=%async_computation.7 | async-start | bytes 786432 | tf_op jit(solution)/shard_map/all_to_all | solution.py:147
  241.3 23.4 %all-to-all-start.6 = ((f32[3,4,1,8192]{3,2,0,1:T(1,128)}), f32[3,4,1,8192]{3,2,0,1:T(1,128)S(1)}, u32[]{:S(2)}, u32[]{:S(2)}) async-start(f32[3,4,1,8192]{3,2,0,1:T(1,128)} %copy.144), calls=%async_computation.6 | async-start | bytes 786432 | tf_op jit(solution)/shard_map/all_to_all | solution.py:146
  272.5 21.9 %all-to-all-start.8 = ((f32[3,4,1,8192]{3,2,0,1:T(1,128)}), f32[3,4,1,8192]{3,2,0,1:T(1,128)S(1)}, u32[]{:S(2)}, u32[]{:S(2)}) async-start(f32[3,4,1,8192]{3,2,0,1:T(1,128)} %reshape.660), calls=%async_computation.8 | async-start | bytes 786432 | tf_op jit(solution)/shard_map/all_to_all | solution.py:115
  294.4 21.5 %all-to-all-start.9 = ((f32[3,4,1,8192]{3,2,0,1:T(1,128)}), f32[3,4,1,8192]{3,2,0,1:T(1,128)S(1)}, u32[]{:S(2)}, u32[]{:S(2)}) async-start(f32[3,4,1,8192]{3,2,0,1:T(1,128)} %reshape.661), calls=%async_computation.9 | async-start | bytes 786432 | tf_op jit(solution)/shard_map/all_to_all | solution.py:114
  320.2 45.1 %all-to-all-start.10 = ((f32[3,128,1,256]{3,2,0,1:T(1,128)}), f32[3,128,1,256]{3,2,0,1:T(1,128)S(1)}, u32[]{:S(2)}, u32[]{:S(2)}) async-start(f32[3,128,1,256]{3,2,0,1:T(1,128)} %copy.157), calls=%async_computation.10 | async-start | bytes 786432 | tf_op jit(solution)/shard_map/all_to_all | solution.py:124
  365.3 33.7 %all-to-all-start.11 = ((f32[3,128,1,256]{3,2,0,1:T(1,128)}), f32[3,128,1,256]{3,2,0,1:T(1,128)S(1)}, u32[]{:S(2)}, u32[]{:S(2)}) async-start(f32[3,128,1,256]{3,2,0,1:T(1,128)} %copy.160), calls=%async_computation.11 | async-start | bytes 786432 | tf_op jit(solution)/shard_map/all_to_all | solution.py:123
  403.9 0.7 copy-start.1
  408.4 27.9 %all-to-all-start.13 = ((f32[2,128,1,256]{3,0,2,1:T(2,128)}), f32[2,128,1,256]{3,0,2,1:T(2,128)S(1)}, u32[]{:S(2)}, u32[]{:S(2)}) async-start(f32[2,128,1,256]{3,0,2,1:T(2,128)} %copy.165), calls=%async_computation.13 | async-start | bytes 524288 | tf_op jit(solution)/shard_map/all_to_all | solution.py:138
  436.3 28.0 %all-to-all-start.12 = ((f32[2,128,1,256]{3,0,2,1:T(2,128)}), f32[2,128,1,256]{3,0,2,1:T(2,128)S(1)}, u32[]{:S(2)}, u32[]{:S(2)}) async-start(f32[2,128,1,256]{3,0,2,1:T(2,128)} %copy.162), calls=%async_computation.12 | async-start | bytes 524288 | tf_op jit(solution)/shard_map/all_to_all | solution.py:137
  467.7 28.4 %all-to-all-start.15 = ((f32[2,4,1,8192]{3,0,2,1:T(2,128)}), f32[2,4,1,8192]{3,0,2,1:T(2,128)S(1)}, u32[]{:S(2)}, u32[]{:S(2)}) async-start(f32[2,4,1,8192]{3,0,2,1:T(2,128)} %copy.170), calls=%async_computation.15 | async-start | bytes 524288 | tf_op jit(solution)/shard_map/all_to_all | solution.py:147
  496.1 21.4 %all-to-all-start.14 = ((f32[2,4,1,8192]{3,0,2,1:T(2,128)}), f32[2,4,1,8192]{3,0,2,1:T(2,128)S(1)}, u32[]{:S(2)}, u32[]{:S(2)}) async-start(f32[2,4,1,8192]{3,0,2,1:T(2,128)} %copy.168), calls=%async_computation.14 | async-start | bytes 524288 | tf_op jit(solution)/shard_map/all_to_all | solution.py:146
where the time goes:
time: 531 us; the launch traced here: 523 us
  waiting for transfers between devices  280 us (53%)
  starting transfers between devices  139 us (26%)
  matrix products  61.9 us (12%)
  local copies, waits for them, and re-layouts  37.6 us (7%)
    dot_general x32, matrix products, times_left(): return jnp.matmul(table, field, precision=lax.Precision.HIGHEST)  50.5 us
    all_to_all x2, waiting for transfers between devices, inverse(): lax.all_to_all(imag_part, 'gy', split_axis=1, concat_axis=2, tiled=True)  41.6 us
    all_to_all x2, waiting for transfers between devices, inverse(): lax.all_to_all(real_part, ('gx', 'gz'), split_axis=1, concat_axis=2, tile...  37.4 us
    all_to_all x2, waiting for transfers between devices, forward(): lax.all_to_all(real_part, ('gx', 'gz'), split_axis=1, concat_axis=2, tile...  36.9 us
    all_to_all x2, waiting for transfers between devices, forward(): lax.all_to_all(imag_part, ('gx', 'gz'), split_axis=1, concat_axis=2, tile...  35.8 us
    all_to_all x2, waiting for transfers between devices, inverse(): lax.all_to_all(imag_part, ('gx', 'gz'), split_axis=1, concat_axis=2, tile...  35 us
    all_to_all x2, waiting for transfers between devices, forward(): lax.all_to_all(real_part, 'gy', split_axis=1, concat_axis=2, tiled=True)  34.2 us
    all_to_all x2, waiting for transfers between devices, inverse(): lax.all_to_all(real_part, 'gy', split_axis=1, concat_axis=2, tiled=True)  31.5 us
  transfers between devices with their start and end apart: 16, of which 16 were waited for; matrix products, arithmetic and copies ran while one was open for 10% of the time, Pallas kernels for 0%

commit v1 on v0

v1 whole, which is shorter than its diff:
```python
import functools

import jax
import jax.numpy as jnp
import numpy as np
from jax import lax
from jax.experimental import pallas as pl
from jax.experimental.pallas import tpu as pltpu
from jax.sharding import PartitionSpec as P

MESH = pl.DeviceIdType.MESH

N = 256
step_chemo = 1.0e-4
step_motile = 2.0e-4
step_diffuse = 2.0e-4
step_secrete = 0.5
step_decay = 0.1

GROUP = 16
ROWS = 256
LANES = 128


def tables():
    index = np.arange(N)
    gap = (index[:, None] - index[None, :]) % N
    wave = np.arange(1, N // 2)
    row = -(2.0 / N) * np.sum(
        wave[:, None] * np.sin(2.0 * np.pi * ((wave[:, None] * index[None, :]) % N) / N), axis=0
    )
    deriv = row[gap]
    angle = 2.0 * np.pi * ((index[:, None] * index[None, :]) % N) / N
    hartley = (np.cos(angle) + np.sin(angle)) / np.sqrt(N)
    place = np.arange(N)
    x2, zl, yc, xc = place // 128, (place // 16) % 8, (place // 4) % 4, place % 4
    order_x = 2 * (yc * 32 + zl * 4 + xc) + x2
    order_y = ((place // 64) % 2) * 128 + (place // 128) * 64 + place % 64
    pick = lambda m, o: m[o][:, o]
    mats = (
        deriv, hartley,
        pick(deriv, order_x), pick(hartley, order_x),
        pick(deriv, order_y).T, pick(hartley, order_y),
    )
    half = np.minimum(index, N - index).astype(np.float64) ** 2
    return [np.asarray(m, np.float32) for m in mats], half[order_x], half[order_y]


def dot(a, b):
    return jnp.dot(a, b, precision=lax.Precision.HIGHEST, preferred_element_type=jnp.float32)


def block(ref, i):
    return ref.at[pl.ds(pl.multiple_of(i * GROUP, GROUP), GROUP), :]


def regroup(src, dst):
    for j in range(GROUP):
        dst[pl.ds(j * GROUP, GROUP), :] = src[pl.ds(j, GROUP, stride=GROUP), :]


def to_plane(m):
    a, b = m[:128], m[128:]
    low = lax.broadcasted_iota(jnp.int32, (128, 128), 1) < 64
    turn = lambda v: pltpu.roll(v, 64, 1)
    return jnp.concatenate([jnp.where(low, a, turn(b)), jnp.where(low, turn(a), b)], axis=0)


def kernel(
    dens_ref, pher_ref, dz, hz, dx, hx, dy, hy, mx_ref, my_ref,
    out_d, out_p,
    buf, full, base, filt, send_sem, recv_sem, core_send, core_recv,
):
    gx, gy, gz = lax.axis_index("gx"), lax.axis_index("gy"), lax.axis_index("gz")
    xc, yc, core = gz % 4, gx, gy % 2
    zc = (gy // 2) * 8 + gz // 4
    col = yc * 4 + xc

    def device(x, y, z, c):
        return (y, (z // 8) * 2 + c, (z % 8) * 4 + x)

    def peer(kind, i):
        if kind == "z":
            far = 8 - i // 2
            z = lax.rem(zc + 16 + jnp.where(i % 2 == 1, far, -far), 16)
            return z, device(xc, yc, z, core)
        y, x = (yc + i // 4) % 4, (xc + i % 4) % 4
        return y * 4 + x, device(x, y, zc, core)

    sibling = device(xc, yc, zc, 1 - core)
    barrier = pltpu.get_barrier_semaphore()
    for kind in ("z", "xy"):
        def greet(i, carry, kind=kind):
            pl.semaphore_signal(barrier, inc=1, device_id=peer(kind, i)[1], device_id_type=MESH)
            return carry
        lax.fori_loop(1, GROUP, greet, 0)
    pl.semaphore_signal(barrier, inc=1, device_id=sibling, device_id_type=MESH)

    def start(kind, src, dst, n):
        mine = zc if kind == "z" else col
        target = block(buf.at[dst], mine)
        def send(i, carry):
            number, where = peer(kind, i)
            pltpu.make_async_remote_copy(
                src_ref=block(buf.at[src], number), dst_ref=target,
                send_sem=send_sem.at[n], recv_sem=recv_sem.at[n],
                device_id=where, device_id_type=MESH,
            ).start()
            return carry
        lax.fori_loop(1, GROUP, send, 0)
        pltpu.make_async_copy(block(buf.at[src], mine), target, recv_sem.at[n]).start()

    def arrived(dst, n):
        pltpu.make_async_copy(buf.at[dst], buf.at[dst], recv_sem.at[n]).wait()

    FIRST = {"out": "xy", "back": "z"}
    SECOND = {"out": "z", "back": "xy"}

    def leave(trip, way, value):
        buf[4 * trip] = value
        start(FIRST[way], 4 * trip, 4 * trip + 1, 2 * trip)

    def forward(trip, way):
        arrived(4 * trip + 1, 2 * trip)
        regroup(buf.at[4 * trip + 1], buf.at[4 * trip + 2])
        start(SECOND[way], 4 * trip + 2, 4 * trip + 3, 2 * trip + 1)

    def land(trip):
        arrived(4 * trip + 3, 2 * trip + 1)
        return buf[4 * trip + 3]

    def share(k, value):
        full[k, core] = value
        pltpu.make_async_remote_copy(
            src_ref=full.at[k, core], dst_ref=full.at[k, core],
            send_sem=core_send.at[k], recv_sem=core_recv.at[k],
            device_id=sibling, device_id_type=MESH,
        ).start()

    def shared(k):
        other = full.at[k, 1 - core]
        pltpu.make_async_copy(other, other, core_recv.at[k]).wait()
        return jnp.concatenate([full[k, 0], full[k, 1]], axis=1)

    own = pl.ds(pl.multiple_of(core * LANES, LANES), LANES)
    RHO, CHEM, PLUS, TERM, PLUS_BACK, MOVED, MOVED_BACK = range(7)

    rho = dens_ref[...].T
    chem = pher_ref[...].T
    pl.semaphore_wait(barrier, 2 * (GROUP - 1) + 1)
    leave(RHO, "out", rho)
    leave(CHEM, "out", chem)
    leave(PLUS, "out", dot(hz[...], chem + step_secrete * rho))
    forward(RHO, "out")
    forward(CHEM, "out")
    base[...] = rho - step_chemo * dot(dz[...], rho * dot(dz[...], chem))
    forward(PLUS, "out")
    wave = (col * GROUP + zc).astype(jnp.float32)
    wave = jnp.minimum(wave, N - wave)
    ksquare = mx_ref[...] + my_ref[...] + wave * wave
    filt[0] = 1.0 / (1.0 + step_motile * ksquare)
    filt[1] = 1.0 / (1.0 + step_diffuse * ksquare + step_decay)

    rho_own = to_plane(land(RHO))
    share(0, rho_own)
    chem_own = to_plane(land(CHEM))
    share(1, chem_own)
    term = dot(dx[...], rho_own * dot(dx[...], chem_own))
    rho_all, chem_all = shared(0), shared(1)
    term = term + dot(rho_all * dot(chem_all, dy[...]), dy[:, own])
    leave(TERM, "back", to_plane(term))

    def solve(which, plane):
        modes = dot(dot(hx[...], plane), hy[...]) * filt[which]
        return to_plane(dot(hx[...], dot(modes, hy[:, own])))

    share(2, to_plane(land(PLUS)))
    forward(TERM, "back")
    leave(PLUS_BACK, "back", solve(1, shared(2)))
    moved = base[...] - step_chemo * land(TERM)
    leave(MOVED, "out", dot(hz[...], moved))
    forward(PLUS_BACK, "back")
    forward(MOVED, "out")
    out_p[...] = dot(hz[...], land(PLUS_BACK)).T
    share(3, to_plane(land(MOVED)))
    leave(MOVED_BACK, "back", solve(0, shared(3)))
    forward(MOVED_BACK, "back")
    out_d[...] = dot(hz[...], land(MOVED_BACK)).T

    def sent(n, carry):
        pltpu.make_async_copy(
            buf.at[0, pl.ds(0, ROWS - GROUP)], buf.at[0, pl.ds(0, ROWS - GROUP)], send_sem.at[n]
        ).wait()
        return carry
    lax.fori_loop(0, 14, sent, 0)
    def core_sent(k, carry):
        pltpu.make_async_copy(full.at[0, 0], full.at[0, 0], core_send.at[k]).wait()
        return carry
    lax.fori_loop(0, 4, core_sent, 0)


def per_device(density, pheromone):
    mats, mx, my = tables()
    mx = np.asarray(np.broadcast_to(mx[:, None], (N, N)), np.float32)
    my = np.asarray(np.broadcast_to(my[None, :], (8, N))[:1], np.float32)
    vmem = pl.BlockSpec(memory_space=pltpu.VMEM)
    flat = jax.ShapeDtypeStruct((LANES, N), jnp.float32)
    new_d, new_p = pl.pallas_call(
        kernel,
        out_shape=(flat, flat),
        in_specs=[vmem] * 10,
        out_specs=(vmem, vmem),
        scratch_shapes=[
            pltpu.VMEM((28, ROWS, LANES), jnp.float32),
            pltpu.VMEM((4, 2, N, LANES), jnp.float32),
            pltpu.VMEM((ROWS, LANES), jnp.float32),
            pltpu.VMEM((2, N, N), jnp.float32),
            pltpu.SemaphoreType.DMA((14,)),
            pltpu.SemaphoreType.DMA((14,)),
            pltpu.SemaphoreType.DMA((4,)),
            pltpu.SemaphoreType.DMA((4,)),
        ],
        compiler_params=pltpu.CompilerParams(
            collective_id=0, has_side_effects=True, vmem_limit_bytes=40 << 20
        ),
        name="chemotaxis_step",
    )(density.reshape(LANES, N), pheromone.reshape(LANES, N), *mats, mx, my)
    return new_d.reshape(density.shape), new_p.reshape(density.shape)


def solution(mesh):
    placed = (P(("gx", "gz"), "gy", None), P(("gx", "gz"), "gy", None))
    return jax.shard_map(
        per_device, mesh=mesh, in_specs=placed, out_specs=placed, check_vma=False
    )
```

time: 531 us -> 99.2 us (0.19)
  the two profiles are of different devices: /device:TPU:33 before, /device:TPU:1 now
where the time goes in v1:
time: 99.2 us; the launch traced here: 98.8 us
  Pallas kernels  87.7 us (88%)
  local copies, waits for them, and re-layouts  10.4 us (10%)
    pallas_call x1, Pallas kernels, per_device(): pl.pallas_call(kernel, out_shape=(flat, flat), in_specs=[vmem] * 10, out_...  87.7 us
    unnamed x22, local copies, waits for them, and re-layouts  10.4 us

profile of v1, /device:TPU:1, one launch (start us, length us, event | category | flops | bytes accessed | tf_op | source)
XLA Modules:
  0.0 98.8 jit_solution(17889544753052714037)
XLA Ops:
  0.6 0.0 copy-start.9
  0.6 0.7 copy-done.9
  1.3 0.0 copy-start
  1.3 0.9 copy-done
  2.3 0.0 copy-start.1
  2.3 0.9 copy-done.1
  3.2 0.0 copy-start.2
  3.2 0.9 copy-done.2
  4.2 0.0 copy-start.3
  4.2 0.9 copy-done.3
  5.1 0.0 copy-start.4
  5.1 0.9 copy-done.4
  6.1 0.0 copy-start.5
  6.1 0.9 copy-done.5
  7.0 0.0 copy-start.6
  7.0 0.9 copy-done.6
  8.0 0.0 copy-start.7
  8.0 0.9 copy-done.7
  8.9 0.0 copy-start.8
  8.9 0.9 copy-done.8
  9.8 87.7 %chemotaxis_step.1 = (f32[128,256]{1,0:T(8,128)S(1)}, f32[128,256]{1,0:T(8,128)S(1)}) custom-call(f32[128,256]{1,0:T(8,128)S(1)} %bitcast.6, f32[128,256]{1,0:T(8,128)S(1)} %bitcast.7, f32[256,256]{1,0:T(8,128)S(1)} %copy-done.6, f32[256,256]{1,0:T(8,128)S(1)} %copy-done.5, f32[256,256]{1,0:T(8,128)S(1)} %copy-done.4, f32[256,256]{1,0:T(8,128)S(1)} %copy-done.3, ...), custom_call_target="tpu_custom_call" | custom-call | tf_op jit(solution)/shard_map/chemotaxis_step/pallas_call | solution.py:208
  97.5 0.7 copy.14
  98.2 0.7 copy.15
Async XLA Ops:
  0.6 0.7 copy-start.9
  1.3 0.9 copy-start
  2.3 0.9 copy-start.1
  3.2 0.9 copy-start.2
  4.2 0.9 copy-start.3
  5.1 0.9 copy-start.4
  6.1 0.9 copy-start.5
  7.0 0.9 copy-start.6
  8.0 0.9 copy-start.7
  8.9 0.9 copy-start.8

commit v2 on v1

--- a/solution.py
+++ b/solution.py
@@ -67,10 +67,20 @@
 
 
 def kernel(
-    dens_ref, pher_ref, dz, hz, dx, hx, dy, hy, mx_ref, my_ref,
+    dens_ref, pher_ref, mats_ref, marks_ref,
     out_d, out_p,
-    buf, full, base, filt, send_sem, recv_sem, core_send, core_recv,
+    fields, mats, marks, buf, full, base, filt,
+    load_sem, send_sem, recv_sem, core_send, core_recv,
 ):
+    loads = [
+        pltpu.make_async_copy(dens_ref, fields.at[0], load_sem.at[0]),
+        pltpu.make_async_copy(pher_ref, fields.at[1], load_sem.at[1]),
+        pltpu.make_async_copy(mats_ref, mats, load_sem.at[2]),
+        pltpu.make_async_copy(marks_ref, marks, load_sem.at[3]),
+    ]
+    for load in loads:
+        load.start()
+    dz, hz, dx, hx, dy, hy = (mats.at[i] for i in range(6))
     gx, gy, gz = lax.axis_index("gx"), lax.axis_index("gy"), lax.axis_index("gz")
     xc, yc, core = gz % 4, gx, gy % 2
     zc = (gy // 2) * 8 + gz // 4
@@ -145,11 +155,14 @@
     own = pl.ds(pl.multiple_of(core * LANES, LANES), LANES)
     RHO, CHEM, PLUS, TERM, PLUS_BACK, MOVED, MOVED_BACK = range(7)
 
-    rho = dens_ref[...].T
-    chem = pher_ref[...].T
+    loads[0].wait()
+    rho = fields[0].T
+    loads[1].wait()
+    chem = fields[1].T
     pl.semaphore_wait(barrier, 2 * (GROUP - 1) + 1)
     leave(RHO, "out", rho)
     leave(CHEM, "out", chem)
+    loads[2].wait()
     leave(PLUS, "out", dot(hz[...], chem + step_secrete * rho))
     forward(RHO, "out")
     forward(CHEM, "out")
@@ -157,7 +170,8 @@
     forward(PLUS, "out")
     wave = (col * GROUP + zc).astype(jnp.float32)
     wave = jnp.minimum(wave, N - wave)
-    ksquare = mx_ref[...] + my_ref[...] + wave * wave
+    loads[3].wait()
+    ksquare = marks[...] + wave * wave
     filt[0] = 1.0 / (1.0 + step_motile * ksquare)
     filt[1] = 1.0 / (1.0 + step_diffuse * ksquare + step_decay)
 
@@ -201,30 +215,34 @@
 
 def per_device(density, pheromone):
     mats, mx, my = tables()
-    mx = np.asarray(np.broadcast_to(mx[:, None], (N, N)), np.float32)
-    my = np.asarray(np.broadcast_to(my[None, :], (8, N))[:1], np.float32)
+    marks = np.asarray(mx[:, None] + my[None, :], np.float32)
+    hbm = pl.BlockSpec(memory_space=pltpu.HBM)
     vmem = pl.BlockSpec(memory_space=pltpu.VMEM)
     flat = jax.ShapeDtypeStruct((LANES, N), jnp.float32)
     new_d, new_p = pl.pallas_call(
         kernel,
         out_shape=(flat, flat),
-        in_specs=[vmem] * 10,
+        in_specs=[hbm] * 4,
         out_specs=(vmem, vmem),
         scratch_shapes=[
+            pltpu.VMEM((2, LANES, N), jnp.float32),
+            pltpu.VMEM((6, N, N), jnp.float32),
+            pltpu.VMEM((N, N), jnp.float32),
             pltpu.VMEM((28, ROWS, LANES), jnp.float32),
             pltpu.VMEM((4, 2, N, LANES), jnp.float32),
             pltpu.VMEM((ROWS, LANES), jnp.float32),
             pltpu.VMEM((2, N, N), jnp.float32),
+            pltpu.SemaphoreType.DMA((4,)),
             pltpu.SemaphoreType.DMA((14,)),
             pltpu.SemaphoreType.DMA((14,)),
             pltpu.SemaphoreType.DMA((4,)),
             pltpu.SemaphoreType.DMA((4,)),
         ],
         compiler_params=pltpu.CompilerParams(
-            collective_id=0, has_side_effects=True, vmem_limit_bytes=40 << 20
+            collective_id=0, has_side_effects=True, vmem_limit_bytes=60 << 20
         ),
         name="chemotaxis_step",
-    )(density.reshape(LANES, N), pheromone.reshape(LANES, N), *mats, mx, my)
+    )(density.reshape(LANES, N), pheromone.reshape(LANES, N), np.stack(mats), marks)
     return new_d.reshape(density.shape), new_p.reshape(density.shape)
 
 

time: 99.2 us -> 92.3 us (0.930)
  local copies, waits for them, and re-layouts: 10.4 us -> 3.14 us
    unnamed x22 -> x2, local copies, waits for them, and re-layouts: 10.4 us -> 3.14 us
where the time goes in v2:
time: 92.3 us; the launch traced here: 92.2 us
  Pallas kernels  88.4 us (96%)
  local copies, waits for them, and re-layouts  3.14 us (3%)
    pallas_call x1, Pallas kernels, per_device(): pl.pallas_call(kernel, out_shape=(flat, flat), in_specs=[hbm] * 4, out_sp...  88.4 us
    unnamed x2, local copies, waits for them, and re-layouts  3.14 us

profile of v2, /device:TPU:1, one launch (start us, length us, event | category | flops | bytes accessed | tf_op | source)
XLA Modules:
  0.0 92.2 jit_solution(17029267540585560547)
XLA Ops:
  0.6 88.4 %chemotaxis_step.1 = (f32[128,256]{1,0:T(8,128)}, f32[128,256]{1,0:T(8,128)}) custom-call(f32[128,256]{1,0:T(8,128)} %bitcast.4, f32[128,256]{1,0:T(8,128)} %bitcast.5, f32[6,256,256]{2,1,0:T(8,128)} %constant.4.clone.mats_ref, f32[256,256]{1,0:T(8,128)} %constant.5.clone.marks_ref), custom_call_target="tpu_custom_call" | custom-call | tf_op jit(solution)/shard_map/chemotaxis_step/pallas_call | solution.py:222
  89.0 1.6 %copy.8 = f32[2,64,256]{2,1,0:T(8,128)} copy(f32[2,64,256]{2,1,0:T(8,128)} %bitcast.7) | data formatting | bytes 262144
  90.6 1.6 %copy.9 = f32[2,64,256]{2,1,0:T(8,128)} copy(f32[2,64,256]{2,1,0:T(8,128)} %bitcast.6) | data formatting | bytes 262144

commit v3 on v2

v3 whole, which is shorter than its diff:
```python
import functools

import jax
import jax.numpy as jnp
import numpy as np
from jax import lax
from jax.experimental import pallas as pl
from jax.experimental.pallas import tpu as pltpu
from jax.sharding import PartitionSpec as P

MESH = pl.DeviceIdType.MESH

N = 256
step_chemo = 1.0e-4
step_motile = 2.0e-4
step_diffuse = 2.0e-4
step_secrete = 0.5
step_decay = 0.1

GROUP = 16
ROWS = 256
LANES = 128


def tables():
    index = np.arange(N)
    gap = (index[:, None] - index[None, :]) % N
    wave = np.arange(1, N // 2)
    row = -(2.0 / N) * np.sum(
        wave[:, None] * np.sin(2.0 * np.pi * ((wave[:, None] * index[None, :]) % N) / N), axis=0
    )
    deriv = row[gap]
    angle = 2.0 * np.pi * ((index[:, None] * index[None, :]) % N) / N
    hartley = (np.cos(angle) + np.sin(angle)) / np.sqrt(N)
    place = np.arange(N)
    x2, zl, yc, xc = place // 128, (place // 16) % 8, (place // 4) % 4, place % 4
    order_x = 2 * (yc * 32 + zl * 4 + xc) + x2
    order_y = ((place // 64) % 2) * 128 + (place // 128) * 64 + place % 64
    pick = lambda m, o: m[o][:, o]
    mats = (
        deriv, hartley,
        pick(deriv, order_x), pick(hartley, order_x),
        pick(deriv, order_y).T, pick(hartley, order_y),
    )
    half = np.minimum(index, N - index).astype(np.float64) ** 2
    return [np.asarray(m, np.float32) for m in mats], half[order_x], half[order_y]


def split(value):
    high = value.astype(jnp.bfloat16)
    return high, (value - high.astype(jnp.float32)).astype(jnp.bfloat16)


def dot(a, b):
    mul = functools.partial(jnp.dot, preferred_element_type=jnp.float32)
    return mul(a[0], b[0]) + (mul(a[0], b[1]) + mul(a[1], b[0]))


def row(ref, i):
    return ref.at[pl.ds(i, 1), :]


def to_plane(m):
    a, b = m[:128], m[128:]
    low = lax.broadcasted_iota(jnp.int32, (128, 128), 1) < 64
    turn = lambda v: pltpu.roll(v, 64, 1)
    return jnp.concatenate([jnp.where(low, a, turn(b)), jnp.where(low, turn(a), b)], axis=0)


def kernel(
    dens_ref, pher_ref, mats_ref, marks_ref,
    out_d, out_p,
    fields, exact, mats, marks, buf, full, base, filt,
    load_sem, send_sem, recv_sem, core_send, core_recv,
):
    loads = [
        pltpu.make_async_copy(dens_ref, fields.at[0], load_sem.at[0]),
        pltpu.make_async_copy(pher_ref, fields.at[1], load_sem.at[1]),
        pltpu.make_async_copy(mats_ref, exact, load_sem.at[2]),
        pltpu.make_async_copy(marks_ref, marks, load_sem.at[3]),
    ]
    for load in loads:
        load.start()
    dz, hz, dx, hx, dy, hy = range(6)

    def table(i):
        return mats[2 * i], mats[2 * i + 1]

    def left(i, value):
        return dot(table(i), split(value))

    def right(value, i):
        return dot(split(value), table(i))

    def right_own(value, i):
        return dot(split(value), (mats[2 * i, :, own], mats[2 * i + 1, :, own]))

    gx, gy, gz = lax.axis_index("gx"), lax.axis_index("gy"), lax.axis_index("gz")
    xc, yc, core = gz % 4, gx, gy % 2
    zc = (gy // 2) * 8 + gz // 4
    col = yc * 4 + xc
    own = pl.ds(pl.multiple_of(core * LANES, LANES), LANES)

    def device(x, y, z, c):
        return (y, (z // 8) * 2 + c, (z % 8) * 4 + x)

    def each_chip(act, mine):
        def some(i, carry):
            far = 8 - i // 4
            y = (yc + 2 + i) % 4
            ahead, behind = (zc + far) % 16, (zc + 17 - far) % 16
            for dx_ in (2, 1, 3, 0):
                x = (xc + dx_) % 4
                act(x, y, ahead)
                if dx_:
                    act(x, y, behind)
                else:
                    here = i == 30
                    pl.when(jnp.logical_not(here))(lambda: act(x, y, behind))
                    pl.when(here)(mine)
            return carry
        lax.fori_loop(0, 32, some, 0)

    sibling = device(xc, yc, zc, 1 - core)
    barrier = pltpu.get_barrier_semaphore()

    def greet(where):
        pl.semaphore_signal(barrier, inc=1, device_id=where, device_id_type=MESH)

    each_chip(lambda x, y, z: greet(device(x, y, z, core)), lambda: greet(sibling))

    def place(way, column, z):
        return column * GROUP + z if way == "out" else z * GROUP + column

    def leave(trip, way, value):
        src, dst = buf.at[2 * trip], buf.at[2 * trip + 1]
        buf[2 * trip] = value
        target = row(dst, zc * GROUP + col if way == "out" else col * GROUP + zc)

        def send(x, y, z):
            pltpu.make_async_remote_copy(
                src_ref=row(src, place(way, y * 4 + x, z)), dst_ref=target,
                send_sem=send_sem.at[trip], recv_sem=recv_sem.at[trip],
                device_id=device(x, y, z, core), device_id_type=MESH,
            ).start()

        def keep():
            pltpu.make_async_copy(row(src, place(way, col, zc)), target, recv_sem.at[trip]).start()

        each_chip(send, keep)

    def land(trip):
        dst = buf.at[2 * trip + 1]
        pltpu.make_async_copy(dst, dst, recv_sem.at[trip]).wait()
        return dst[...]

    def share(k, value):
        full[k, core] = value
        pltpu.make_async_remote_copy(
            src_ref=full.at[k, core], dst_ref=full.at[k, core],
            send_sem=core_send.at[k], recv_sem=core_recv.at[k],
            device_id=sibling, device_id_type=MESH,
        ).start()

    def shared(k):
        other = full.at[k, 1 - core]
        pltpu.make_async_copy(other, other, core_recv.at[k]).wait()
        return jnp.concatenate([full[k, 0], full[k, 1]], axis=1)

    RHO, CHEM, PLUS, TERM, PLUS_BACK, MOVED, MOVED_BACK = range(7)

    loads[0].wait()
    rho = fields[0].T
    loads[1].wait()
    chem = fields[1].T
    loads[2].wait()
    for i in range(6):
        mats[2 * i], mats[2 * i + 1] = split(exact[i])
    pl.semaphore_wait(barrier, ROWS)
    leave(RHO, "out", rho)
    leave(CHEM, "out", chem)
    leave(PLUS, "out", left(hz, chem + step_secrete * rho))
    base[...] = rho - step_chemo * left(dz, rho * left(dz, chem))
    wave = (col * GROUP + zc).astype(jnp.float32)
    wave = jnp.minimum(wave, N - wave)
    loads[3].wait()
    ksquare = marks[...] + wave * wave
    filt[0] = 1.0 / (1.0 + step_motile * ksquare)
    filt[1] = 1.0 / (1.0 + step_diffuse * ksquare + step_decay)

    rho_own = to_plane(land(RHO))
    share(0, rho_own)
    chem_own = to_plane(land(CHEM))
    share(1, chem_own)
    term = left(dx, rho_own * left(dx, chem_own))
    rho_all, chem_all = shared(0), shared(1)
    term = term + right_own(rho_all * right(chem_all, dy), dy)
    leave(TERM, "back", to_plane(term))

    def solve(which, plane):
        modes = right(left(hx, plane), hy) * filt[which]
        return to_plane(left(hx, right_own(modes, hy)))

    share(2, to_plane(land(PLUS)))
    plus = solve(1, shared(2))
    leave(MOVED, "out", left(hz, base[...] - step_chemo * land(TERM)))
    leave(PLUS_BACK, "back", plus)
    share(3, to_plane(land(MOVED)))
    leave(MOVED_BACK, "back", solve(0, shared(3)))
    out_p[...] = left(hz, land(PLUS_BACK)).T
    out_d[...] = left(hz, land(MOVED_BACK)).T

    def sent(n, carry):
        rest = buf.at[0, pl.ds(0, ROWS - 1), :]
        pltpu.make_async_copy(rest, rest, send_sem.at[n]).wait()
        return carry
    lax.fori_loop(0, 7, sent, 0)
    def core_sent(k, carry):
        pltpu.make_async_copy(full.at[0, 0], full.at[0, 0], core_send.at[k]).wait()
        return carry
    lax.fori_loop(0, 4, core_sent, 0)


def per_device(density, pheromone):
    mats, mx, my = tables()
    marks = np.asarray(mx[:, None] + my[None, :], np.float32)
    hbm = pl.BlockSpec(memory_space=pltpu.HBM)
    vmem = pl.BlockSpec(memory_space=pltpu.VMEM)
    flat = jax.ShapeDtypeStruct((LANES, N), jnp.float32)
    new_d, new_p = pl.pallas_call(
        kernel,
        out_shape=(flat, flat),
        in_specs=[hbm] * 4,
        out_specs=(vmem, vmem),
        scratch_shapes=[
            pltpu.VMEM((2, LANES, N), jnp.float32),
            pltpu.VMEM((6, N, N), jnp.float32),
            pltpu.VMEM((12, N, N), jnp.bfloat16),
            pltpu.VMEM((N, N), jnp.float32),
            pltpu.VMEM((14, ROWS, LANES), jnp.float32),
            pltpu.VMEM((4, 2, N, LANES), jnp.float32),
            pltpu.VMEM((ROWS, LANES), jnp.float32),
            pltpu.VMEM((2, N, N), jnp.float32),
            pltpu.SemaphoreType.DMA((4,)),
            pltpu.SemaphoreType.DMA((7,)),
            pltpu.SemaphoreType.DMA((7,)),
            pltpu.SemaphoreType.DMA((4,)),
            pltpu.SemaphoreType.DMA((4,)),
        ],
        compiler_params=pltpu.CompilerParams(
            collective_id=0, has_side_effects=True, vmem_limit_bytes=60 << 20
        ),
        name="chemotaxis_step",
    )(density.reshape(LANES, N), pheromone.reshape(LANES, N), np.stack(mats), marks)
    return new_d.reshape(density.shape), new_p.reshape(density.shape)


def solution(mesh):
    placed = (P(("gx", "gz"), "gy", None), P(("gx", "gz"), "gy", None))
    return jax.shard_map(
        per_device, mesh=mesh, in_specs=placed, out_specs=placed, check_vma=False
    )
```

time: 92.3 us -> 80.6 us (0.87)
  Pallas kernels: 88.4 us -> 76.7 us
    pallas_call x1, Pallas kernels: 88.4 us -> 76.7 us  [per_device(): pl.pallas_call(kernel, out_shape=(flat, flat), in_specs=[hbm] * 4, out_sp...]
where the time goes in v3:
time: 80.6 us; the launch traced here: 80.5 us
  Pallas kernels  76.7 us (95%)
  local copies, waits for them, and re-layouts  3.14 us (4%)
    pallas_call x1, Pallas kernels, per_device(): pl.pallas_call(kernel, out_shape=(flat, flat), in_specs=[hbm] * 4, out_sp...  76.7 us
    unnamed x2, local copies, waits for them, and re-layouts  3.14 us

profile of v3, /device:TPU:1, one launch (start us, length us, event | category | flops | bytes accessed | tf_op | source)
XLA Modules:
  0.0 80.5 jit_solution(15790890086503326102)
XLA Ops:
  0.6 76.7 %chemotaxis_step.1 = (f32[128,256]{1,0:T(8,128)}, f32[128,256]{1,0:T(8,128)}) custom-call(f32[128,256]{1,0:T(8,128)} %bitcast.4, f32[128,256]{1,0:T(8,128)} %bitcast.5, f32[6,256,256]{2,1,0:T(8,128)} %constant.4.clone.mats_ref, f32[256,256]{1,0:T(8,128)} %constant.5.clone.marks_ref), custom_call_target="tpu_custom_call" | custom-call | tf_op jit(solution)/shard_map/chemotaxis_step/pallas_call | solution.py:230
  77.3 1.6 %copy.8 = f32[2,64,256]{2,1,0:T(8,128)} copy(f32[2,64,256]{2,1,0:T(8,128)} %bitcast.7) | data formatting | bytes 262144
  78.9 1.6 %copy.9 = f32[2,64,256]{2,1,0:T(8,128)} copy(f32[2,64,256]{2,1,0:T(8,128)} %bitcast.6) | data formatting | bytes 262144

commit v4 on v3

--- a/solution.py
+++ b/solution.py
@@ -56,6 +56,10 @@
     return mul(a[0], b[0]) + (mul(a[0], b[1]) + mul(a[1], b[0]))
 
 
+def block(ref, i):
+    return ref.at[pl.ds(pl.multiple_of(i * GROUP, GROUP), GROUP), :]
+
+
 def row(ref, i):
     return ref.at[pl.ds(i, 1), :]
 
@@ -69,9 +73,9 @@
 
 def kernel(
     dens_ref, pher_ref, mats_ref, marks_ref,
-    out_d, out_p,
-    fields, exact, mats, marks, buf, full, base, filt,
-    load_sem, send_sem, recv_sem, core_send, core_recv,
+    out,
+    fields, exact, mats, marks, buf, mid, turned, final, full, base, filt,
+    load_sem, store_sem, mid_send, mid_recv, send_sem, recv_sem, core_send, core_recv, ready,
 ):
     loads = [
         pltpu.make_async_copy(dens_ref, fields.at[0], load_sem.at[0]),
@@ -127,7 +131,17 @@
     def greet(where):
         pl.semaphore_signal(barrier, inc=1, device_id=where, device_id_type=MESH)
 
-    each_chip(lambda x, y, z: greet(device(x, y, z, core)), lambda: greet(sibling))
+    def tell(sem, hops):
+        for way in (hops, GROUP - hops):
+            pl.semaphore_signal(
+                sem, inc=1, device_id=device(xc, yc, (zc + way) % GROUP, core), device_id_type=MESH
+            )
+
+    for i in range(1, GROUP):
+        greet(device((xc + i % 4) % 4, (yc + i // 4) % 4, zc, core))
+    for hops in (4, 3, 2, 1):
+        tell(barrier, hops)
+    greet(sibling)
 
     def place(way, column, z):
         return column * GROUP + z if way == "out" else z * GROUP + column
@@ -149,10 +163,40 @@
 
         each_chip(send, keep)
 
+    def across(field):
+        src, dst = buf.at[2 * field], mid.at[field]
+        target = block(dst, col)
+        for i in range(1, GROUP):
+            y, x = (yc + i // 4) % 4, (xc + i % 4) % 4
+            pltpu.make_async_remote_copy(
+                src_ref=block(src, y * 4 + x), dst_ref=target,
+                send_sem=mid_send.at[field], recv_sem=mid_recv.at[field],
+                device_id=device(x, y, zc, core), device_id_type=MESH,
+            ).start()
+        pltpu.make_async_copy(block(src, col), target, mid_recv.at[field]).start()
+
+    def along(field):
+        pltpu.make_async_copy(mid.at[field], mid.at[field], mid_recv.at[field]).wait()
+        src, dst = turned.at[field], buf.at[2 * field + 1]
+        for z in range(GROUP):
+            src[pl.ds(z * GROUP, GROUP), :] = mid[field, pl.ds(z, GROUP, stride=GROUP), :]
+        target = block(dst, zc)
+        for hops in (8, 9, 7, 10, 6, 11, 5, 12, 4, 13, 3, 14, 2, 15, 1):
+            z = (zc + hops) % GROUP
+            pltpu.make_async_remote_copy(
+                src_ref=block(src, z), dst_ref=target,
+                send_sem=send_sem.at[field], recv_sem=recv_sem.at[field],
+                device_id=device(xc, yc, z, core), device_id_type=MESH,
+            ).start()
+        pltpu.make_async_copy(block(src, zc), target, recv_sem.at[field]).start()
+
     def land(trip):
         dst = buf.at[2 * trip + 1]
         pltpu.make_async_copy(dst, dst, recv_sem.at[trip]).wait()
-        return dst[...]
+        return dst
+
+    def landed(trip):
+        return land(trip)[...]
 
     def share(k, value):
         full[k, core] = value
@@ -165,9 +209,13 @@
     def shared(k):
         other = full.at[k, 1 - core]
         pltpu.make_async_copy(other, other, core_recv.at[k]).wait()
-        return jnp.concatenate([full[k, 0], full[k, 1]], axis=1)
-
-    RHO, CHEM, PLUS, TERM, PLUS_BACK, MOVED, MOVED_BACK = range(7)
+        return other[...]
+
+    def joined(mine, other):
+        first = core == 0
+        return jnp.concatenate([jnp.where(first, mine, other), jnp.where(first, other, mine)], axis=1)
+
+    CHEM, RHO, PLUS, TERM, PLUS_BACK, MOVED, MOVED_BACK = range(7)
 
     loads[0].wait()
     rho = fields[0].T
@@ -176,10 +224,19 @@
     loads[2].wait()
     for i in range(6):
         mats[2 * i], mats[2 * i + 1] = split(exact[i])
-    pl.semaphore_wait(barrier, ROWS)
-    leave(RHO, "out", rho)
-    leave(CHEM, "out", chem)
-    leave(PLUS, "out", left(hz, chem + step_secrete * rho))
+    buf[2 * RHO] = rho
+    buf[2 * CHEM] = chem
+    pl.semaphore_wait(barrier, 24)
+    for hops in (4, 3, 2, 1):
+        tell(ready.at[0], hops)
+    for field in (CHEM, RHO):
+        across(field)
+    pl.semaphore_wait(ready.at[0], 8)
+    tell(ready.at[1], 4)
+    for field in (CHEM, RHO):
+        along(field)
+    pl.semaphore_wait(ready.at[1], 2)
+    plus = left(hz, chem + step_secrete * rho)
     base[...] = rho - step_chemo * left(dz, rho * left(dz, chem))
     wave = (col * GROUP + zc).astype(jnp.float32)
     wave = jnp.minimum(wave, N - wave)
@@ -188,70 +245,133 @@
     filt[0] = 1.0 / (1.0 + step_motile * ksquare)
     filt[1] = 1.0 / (1.0 + step_diffuse * ksquare + step_decay)
 
-    rho_own = to_plane(land(RHO))
-    share(0, rho_own)
-    chem_own = to_plane(land(CHEM))
-    share(1, chem_own)
-    term = left(dx, rho_own * left(dx, chem_own))
-    rho_all, chem_all = shared(0), shared(1)
-    term = term + right_own(rho_all * right(chem_all, dy), dy)
+    chem_own = to_plane(landed(CHEM))
+    share(0, chem_own)
+    leave(PLUS, "out", plus)
+    slope_x = left(dx, chem_own)
+    chem_other = shared(0)
+    slope_y = right(joined(chem_own, chem_other), dy)
+    rho_own = to_plane(landed(RHO))
+    share(1, rho_own)
+    term = left(dx, rho_own * slope_x)
+    rho_other = shared(1)
+    term = term + right_own(joined(rho_own, rho_other) * slope_y, dy)
     leave(TERM, "back", to_plane(term))
 
-    def solve(which, plane):
-        modes = right(left(hx, plane), hy) * filt[which]
+    def solve(which, k, trip):
+        mine = to_plane(landed(trip))
+        share(k, mine)
+        mine = left(hx, mine)
+        other = left(hx, shared(k))
+        modes = right(joined(mine, other), hy) * filt[which]
         return to_plane(left(hx, right_own(modes, hy)))
 
-    share(2, to_plane(land(PLUS)))
-    plus = solve(1, shared(2))
-    leave(MOVED, "out", left(hz, base[...] - step_chemo * land(TERM)))
+    plus = solve(1, 2, PLUS)
+    leave(MOVED, "out", left(hz, base[...] - step_chemo * landed(TERM)))
     leave(PLUS_BACK, "back", plus)
-    share(3, to_plane(land(MOVED)))
-    leave(MOVED_BACK, "back", solve(0, shared(3)))
-    out_p[...] = left(hz, land(PLUS_BACK)).T
-    out_d[...] = left(hz, land(MOVED_BACK)).T
-
-    def sent(n, carry):
-        rest = buf.at[0, pl.ds(0, ROWS - 1), :]
-        pltpu.make_async_copy(rest, rest, send_sem.at[n]).wait()
-        return carry
-    lax.fori_loop(0, 7, sent, 0)
+    leave(MOVED_BACK, "back", solve(0, 3, MOVED))
+
+    def store(i, trip):
+        final[i] = left(hz, landed(trip)).T
+        move = pltpu.make_async_copy(final.at[i], out.at[i], store_sem.at[i])
+        move.start()
+        return move
+
+    stores = [store(1, PLUS_BACK), store(0, MOVED_BACK)]
+
+    def sent(sem, count):
+        rest = buf.at[0, pl.ds(0, count), :]
+        pltpu.make_async_copy(rest, rest, sem).wait()
+
+    for field in (CHEM, RHO):
+        sent(mid_send.at[field], ROWS - GROUP)
+        sent(send_sem.at[field], ROWS - GROUP)
+    for trip in (PLUS, TERM, PLUS_BACK, MOVED, MOVED_BACK):
+        sent(send_sem.at[trip], ROWS - 1)
     def core_sent(k, carry):
         pltpu.make_async_copy(full.at[0, 0], full.at[0, 0], core_send.at[k]).wait()
         return carry
     lax.fori_loop(0, 4, core_sent, 0)
+    for store in stores:
+        store.wait()
+
+
+CHUNK = 32
+
+
+def finish(both_ref, dens_ref, pher_ref, held, in_sem, out_sem):
+    parts = [(i, k) for i in range(2) for k in range(LANES // CHUNK)]
+
+    def load(n, i, k):
+        rows = pl.ds(k * CHUNK, CHUNK)
+        return pltpu.make_async_copy(both_ref.at[i, rows, :], held.at[i, rows, :], in_sem.at[n])
+
+    def store(n, i, k):
+        rows = pl.ds(k * CHUNK, CHUNK)
+        target = (dens_ref, pher_ref)[i]
+        return pltpu.make_async_copy(held.at[i, rows, :], target.at[rows, :], out_sem.at[n])
+
+    for n, (i, k) in enumerate(parts):
+        load(n, i, k).start()
+    for n, (i, k) in enumerate(parts):
+        load(n, i, k).wait()
+        store(n, i, k).start()
+    for n, (i, k) in enumerate(parts):
+        store(n, i, k).wait()
 
 
 def per_device(density, pheromone):
     mats, mx, my = tables()
     marks = np.asarray(mx[:, None] + my[None, :], np.float32)
     hbm = pl.BlockSpec(memory_space=pltpu.HBM)
-    vmem = pl.BlockSpec(memory_space=pltpu.VMEM)
     flat = jax.ShapeDtypeStruct((LANES, N), jnp.float32)
-    new_d, new_p = pl.pallas_call(
+    mats = np.stack(mats)
+    both = pl.pallas_call(
         kernel,
-        out_shape=(flat, flat),
+        out_shape=jax.ShapeDtypeStruct((2, LANES, N), jnp.float32),
         in_specs=[hbm] * 4,
-        out_specs=(vmem, vmem),
+        out_specs=hbm,
         scratch_shapes=[
             pltpu.VMEM((2, LANES, N), jnp.float32),
             pltpu.VMEM((6, N, N), jnp.float32),
             pltpu.VMEM((12, N, N), jnp.bfloat16),
             pltpu.VMEM((N, N), jnp.float32),
             pltpu.VMEM((14, ROWS, LANES), jnp.float32),
+            pltpu.VMEM((2, ROWS, LANES), jnp.float32),
+            pltpu.VMEM((2, ROWS, LANES), jnp.float32),
+            pltpu.VMEM((2, LANES, N), jnp.float32),
             pltpu.VMEM((4, 2, N, LANES), jnp.float32),
             pltpu.VMEM((ROWS, LANES), jnp.float32),
             pltpu.VMEM((2, N, N), jnp.float32),
             pltpu.SemaphoreType.DMA((4,)),
+            pltpu.SemaphoreType.DMA((2,)),
+            pltpu.SemaphoreType.DMA((2,)),
+            pltpu.SemaphoreType.DMA((2,)),
             pltpu.SemaphoreType.DMA((7,)),
             pltpu.SemaphoreType.DMA((7,)),
             pltpu.SemaphoreType.DMA((4,)),
             pltpu.SemaphoreType.DMA((4,)),
+            pltpu.SemaphoreType.REGULAR((2,)),
         ],
         compiler_params=pltpu.CompilerParams(
             collective_id=0, has_side_effects=True, vmem_limit_bytes=60 << 20
         ),
         name="chemotaxis_step",
-    )(density.reshape(LANES, N), pheromone.reshape(LANES, N), np.stack(mats), marks)
+    )(density.reshape(LANES, N), pheromone.reshape(LANES, N), mats, marks)
+    flat = jax.ShapeDtypeStruct((LANES, N), jnp.float32)
+    new_d, new_p = pl.pallas_call(
+        finish,
+        out_shape=(flat, flat),
+        in_specs=[hbm],
+        out_specs=(hbm, hbm),
+        scratch_shapes=[
+            pltpu.VMEM((2, LANES, N), jnp.float32),
+            pltpu.SemaphoreType.DMA((2 * LANES // CHUNK,)),
+            pltpu.SemaphoreType.DMA((2 * LANES // CHUNK,)),
+        ],
+        compiler_params=pltpu.CompilerParams(vmem_limit_bytes=60 << 20),
+        name="outputs",
+    )(both)
     return new_d.reshape(density.shape), new_p.reshape(density.shape)
 
 

time: 80.6 us -> 78 us (0.968)
  local copies, waits for them, and re-layouts: 3.14 us -> 0 us
    unnamed x2 -> x0, local copies, waits for them, and re-layouts: 3.14 us -> none
    pallas_call x1 -> x2, Pallas kernels: 76.7 us -> 77.2 us  [the longest x1 75.5 us: per_device(): pl.pallas_call(kernel, out_shape=jax.ShapeDtypeStruct((2, LANES, N), jnp....]
where the time goes in v4:
time: 78 us; the launch traced here: 77.8 us
  Pallas kernels  77.2 us (99%)
    pallas_call x1, Pallas kernels, per_device(): pl.pallas_call(kernel, out_shape=jax.ShapeDtypeStruct((2, LANES, N), jnp....  75.5 us
    pallas_call x1, Pallas kernels, per_device(): pl.pallas_call(finish, out_shape=(flat, flat), in_specs=[hbm], out_specs=...  1.63 us

profile of v4, /device:TPU:1, one launch (start us, length us, event | category | flops | bytes accessed | tf_op | source)
XLA Modules:
  0.0 77.8 jit_solution(1179918400061489364)
XLA Ops:
  0.6 75.5 %chemotaxis_step.1.both_ref = f32[2,128,256]{2,1,0:T(8,128)} custom-call(f32[128,256]{1,0:T(8,128)} %bitcast.4, f32[128,256]{1,0:T(8,128)} %bitcast.5, f32[6,256,256]{2,1,0:T(8,128)} %constant.4.clone.mats_ref, f32[256,256]{1,0:T(8,128)} %constant.5.clone.marks_ref), custom_call_target="tpu_custom_call" | custom-call | tf_op jit(solution)/shard_map/chemotaxis_step/pallas_call | solution.py:329
  76.2 1.6 %outputs.1 = (f32[128,256]{1,0:T(8,128)}, f32[128,256]{1,0:T(8,128)}) custom-call(f32[2,128,256]{2,1,0:T(8,128)} %chemotaxis_step.1.both_ref), custom_call_target="tpu_custom_call" | custom-call | tf_op jit(solution)/shard_map/outputs/pallas_call | solution.py:362

commit v5 on v4

--- a/solution.py
+++ b/solution.py
@@ -247,7 +247,6 @@
 
     chem_own = to_plane(landed(CHEM))
     share(0, chem_own)
-    leave(PLUS, "out", plus)
     slope_x = left(dx, chem_own)
     chem_other = shared(0)
     slope_y = right(joined(chem_own, chem_other), dy)
@@ -257,6 +256,7 @@
     rho_other = shared(1)
     term = term + right_own(joined(rho_own, rho_other) * slope_y, dy)
     leave(TERM, "back", to_plane(term))
+    leave(PLUS, "out", plus)
 
     def solve(which, k, trip):
         mine = to_plane(landed(trip))
@@ -266,9 +266,8 @@
         modes = right(joined(mine, other), hy) * filt[which]
         return to_plane(left(hx, right_own(modes, hy)))
 
-    plus = solve(1, 2, PLUS)
     leave(MOVED, "out", left(hz, base[...] - step_chemo * landed(TERM)))
-    leave(PLUS_BACK, "back", plus)
+    leave(PLUS_BACK, "back", solve(1, 2, PLUS))
     leave(MOVED_BACK, "back", solve(0, 3, MOVED))
 
     def store(i, trip):

time: 78 us -> 75.8 us (0.972)
  Pallas kernels: 77.2 us -> 75 us
    pallas_call x1, Pallas kernels: 75.5 us -> 73.3 us  [per_device(): pl.pallas_call(kernel, out_shape=jax.ShapeDtypeStruct((2, LANES, N), jnp....]
where the time goes in v5:
time: 75.8 us; the launch traced here: 75.6 us
  Pallas kernels  75 us (99%)
    pallas_call x1, Pallas kernels, per_device(): pl.pallas_call(kernel, out_shape=jax.ShapeDtypeStruct((2, LANES, N), jnp....  73.3 us
    pallas_call x1, Pallas kernels, per_device(): pl.pallas_call(finish, out_shape=(flat, flat), in_specs=[hbm], out_specs=...  1.63 us

profile of v5, /device:TPU:1, one launch (start us, length us, event | category | flops | bytes accessed | tf_op | source)
XLA Modules:
  0.0 75.6 jit_solution(14852165470163025116)
XLA Ops:
  0.6 73.3 %chemotaxis_step.1.both_ref = f32[2,128,256]{2,1,0:T(8,128)} custom-call(f32[128,256]{1,0:T(8,128)} %bitcast.4, f32[128,256]{1,0:T(8,128)} %bitcast.5, f32[6,256,256]{2,1,0:T(8,128)} %constant.4.clone.mats_ref, f32[256,256]{1,0:T(8,128)} %constant.5.clone.marks_ref), custom_call_target="tpu_custom_call" | custom-call | tf_op jit(solution)/shard_map/chemotaxis_step/pallas_call | solution.py:328
  74.0 1.6 %outputs.1 = (f32[128,256]{1,0:T(8,128)}, f32[128,256]{1,0:T(8,128)}) custom-call(f32[2,128,256]{2,1,0:T(8,128)} %chemotaxis_step.1.both_ref), custom_call_target="tpu_custom_call" | custom-call | tf_op jit(solution)/shard_map/outputs/pallas_call | solution.py:361

commit v6 on v5

--- a/solution.py
+++ b/solution.py
@@ -137,9 +137,10 @@
                 sem, inc=1, device_id=device(xc, yc, (zc + way) % GROUP, core), device_id_type=MESH
             )
 
-    for i in range(1, GROUP):
+    tell(barrier, 4)
+    for i in (10, 9, 11, 6, 14, 8, 2, 5, 7, 13, 15, 4, 12, 1, 3):
         greet(device((xc + i % 4) % 4, (yc + i // 4) % 4, zc, core))
-    for hops in (4, 3, 2, 1):
+    for hops in (3, 2, 1):
         tell(barrier, hops)
     greet(sibling)
 
@@ -219,18 +220,18 @@
 
     loads[0].wait()
     rho = fields[0].T
+    buf[2 * RHO] = rho
     loads[1].wait()
     chem = fields[1].T
-    loads[2].wait()
-    for i in range(6):
-        mats[2 * i], mats[2 * i + 1] = split(exact[i])
-    buf[2 * RHO] = rho
     buf[2 * CHEM] = chem
     pl.semaphore_wait(barrier, 24)
     for hops in (4, 3, 2, 1):
         tell(ready.at[0], hops)
     for field in (CHEM, RHO):
         across(field)
+    loads[2].wait()
+    for i in range(6):
+        mats[2 * i], mats[2 * i + 1] = split(exact[i])
     pl.semaphore_wait(ready.at[0], 8)
     tell(ready.at[1], 4)
     for field in (CHEM, RHO):
@@ -295,7 +296,7 @@
         store.wait()
 
 
-CHUNK = 32
+CHUNK = 64
 
 
 def finish(both_ref, dens_ref, pher_ref, held, in_sem, out_sem):

time: 75.8 us -> 75.7 us (level)
  no operation moved by 1% of the time
where the time goes in v6:
time: 75.7 us; the launch traced here: 75.5 us
  Pallas kernels  74.9 us (99%)
    pallas_call x1, Pallas kernels, per_device(): pl.pallas_call(kernel, out_shape=jax.ShapeDtypeStruct((2, LANES, N), jnp....  73.3 us
    pallas_call x1, Pallas kernels, per_device(): pl.pallas_call(finish, out_shape=(flat, flat), in_specs=[hbm], out_specs=...  1.63 us

profile of v6, /device:TPU:1, one launch (start us, length us, event | category | flops | bytes accessed | tf_op | source)
XLA Modules:
  0.0 75.5 jit_solution(18146172882340404261)
XLA Ops:
  0.6 73.3 %chemotaxis_step.1.both_ref = f32[2,128,256]{2,1,0:T(8,128)} custom-call(f32[128,256]{1,0:T(8,128)} %bitcast.4, f32[128,256]{1,0:T(8,128)} %bitcast.5, f32[6,256,256]{2,1,0:T(8,128)} %constant.4.clone.mats_ref, f32[256,256]{1,0:T(8,128)} %constant.5.clone.marks_ref), custom_call_target="tpu_custom_call" | custom-call | tf_op jit(solution)/shard_map/chemotaxis_step/pallas_call | solution.py:329
  73.9 1.6 %outputs.1 = (f32[128,256]{1,0:T(8,128)}, f32[128,256]{1,0:T(8,128)}) custom-call(f32[2,128,256]{2,1,0:T(8,128)} %chemotaxis_step.1.both_ref), custom_call_target="tpu_custom_call" | custom-call | tf_op jit(solution)/shard_map/outputs/pallas_call | solution.py:362
